TPU v7x, 256 devices: a whole 4x4x8 slice. The times are simulated.
256 devices in a mesh: rep: 16 (over y_hi, z), row: 16 (over x, y_lo, core).
Axes of the slice: x: 4, y: 4 (y_hi: 2, y_lo: 2; y = y_hi * 2 + y_lo), z: 8, core: 2. Of those that a mesh axis runs over, the one named last changes fastest.
Arguments:
- features: bfloat16 [131072, 256], P(('rep', 'row')), may hold values from -6 to 6
- adj_values: bfloat16 [16, 16, 256, 128, 128], P('rep', 'row'), may hold values from -0.109375 to 0.109375
- block_rows: int32 [16, 16, 256], P('rep', 'row'), may hold values from 0 to 63, as said below
- block_cols: int32 [16, 16, 256], P('rep', 'row'), may hold values from 0 to 63
- counts: int32 [16, 16], P('rep', 'row'), may hold values from 42 to 256, as said below
- weight: bfloat16 [256, 256], replicated, may hold values from -0.375 to 0.375
- bias: float32 [256], replicated, may hold values from -3 to 3
- cotangent: bfloat16 [131072, 256], P(('rep', 'row')), may hold values from -6 to 6
Outputs:
- activations: bfloat16 [131072, 256], P(('rep', 'row'))
- grad_features: bfloat16 [131072, 256], P(('rep', 'row'))
- grad_weight: float32 [256, 256], replicated
- grad_bias: float32 [256], replicated
Inputs may be any that keep to these rules, and one draw needn't show every extreme that they name: Within one device's list the pairs (block_rows, block_cols) are distinct, live or not. `counts`: the live entries are the first ones of each list; at least one list is full.
All inputs are finite; a program needn't handle non-finite values.
Results may differ from a plain program's by a relative error of at most 0.028.
Values may be sent and summed in bfloat16 or wider, within the bound.
A program may use at most 128 MiB of HBM per device.

v0:
```python
import functools

import jax
import jax.numpy as jnp
from jax import lax
from jax.experimental import pallas as pl
from jax.experimental.pallas import tpu as pltpu
from jax.sharding import PartitionSpec as P

MESH = pl.DeviceIdType.MESH
BF = jnp.bfloat16
F32 = jnp.float32
B = 128
CAP = 256
RB = 64
PAIRS = 160
NZ = 8
UNROLL = 20
VMEM_LIMIT = 58 * 2**20


def rem(a, n):
    return lax.rem(a, n)


def place():
    r = lax.axis_index("rep")
    i = lax.axis_index("row")
    return lax.div(r, 8), rem(r, 8), lax.div(i, 4), rem(lax.div(i, 2), 2), rem(i, 2)


def device(yh, z, x, yl, c):
    return (yh * 8 + z, x * 4 + yl * 2 + c)


class Links:
    def __init__(self, send_sem, recv_sem):
        self.send_sem, self.recv_sem, self.copies = send_sem, recv_sem, []

    def send(self, src, dst, to):
        k = len(self.copies)
        copy = pltpu.make_async_remote_copy(
            src_ref=src, dst_ref=dst, send_sem=self.send_sem.at[k], recv_sem=self.recv_sem.at[k],
            device_id=to, device_id_type=MESH,
        )
        copy.start()
        self.copies.append(copy)
        return copy

    def finish(self):
        for copy in self.copies:
            copy.wait_send()


def run(*tasks):
    tasks = list(tasks)
    while tasks:
        for task in list(tasks):
            if next(task, "end") == "end":
                tasks.remove(task)


def together(*tasks):
    tasks = list(tasks)
    while tasks:
        for task in list(tasks):
            if next(task, "end") == "end":
                tasks.remove(task)
            else:
                yield


def advance(task, n):
    for _ in range(n):
        next(task, None)


def products(meta, base, adj, source, sums, adj_first):
    def step(t, acc):
        a0, a1 = adj[meta[base, t]], adj[meta[base + 1, t]]
        x0, x1 = source[meta[base + 2, t]], source[meta[base + 3, t]]
        if adj_first:
            left, right = jnp.concatenate([a0, a1], 1), jnp.concatenate([x0, x1], 0)
        else:
            left, right = jnp.concatenate([x0, x1], 1), jnp.concatenate([a0, a1], 0)
        term = jnp.dot(left, right, preferred_element_type=F32)
        acc = jnp.where(meta[base + 4, t] != 0, 0.0, acc) + term
        sums[t] = acc.astype(BF)
        return acc

    def group(g, acc):
        for k in range(UNROLL):
            acc = step(g * UNROLL + k, acc)
        return acc

    acc = jnp.zeros((B, B), F32)
    sums[PAIRS] = jnp.zeros((B, B), BF)
    for g in range(PAIRS // UNROLL):
        acc = lax.fori_loop(g, g + 1, group, acc)
        yield


def sort_kernel(count_ref, rows_ref, cols_ref, out_ref):
    live = (lax.broadcasted_iota(jnp.int32, (1, CAP), 1) < count_ref[0, 0]).astype(F32)
    sub = lax.broadcasted_iota(jnp.int32, (CAP, CAP), 0).astype(F32)
    lane = lax.broadcasted_iota(jnp.int32, (CAP, CAP), 1).astype(F32)
    eye = (sub == lane).astype(F32)
    rows = rows_ref[...].astype(F32)
    cols = cols_ref[...].astype(F32)

    def column(v):
        return jnp.sum(eye * v, axis=1, keepdims=True)

    def order(key, source):
        key = jnp.where(live > 0, key, 64.0)
        key_col = column(key)
        same = jnp.where(key_col == key, 1.0, 0.0)
        rank = jnp.sum(jnp.where(sub < lane, same, 0.0), axis=0, keepdims=True)
        p = sub[:RB]
        n = jnp.sum(jnp.where(p == key, 1.0, 0.0), axis=1, keepdims=True)
        pairs = jnp.floor((n + 1.0) * 0.5)
        base = jnp.sum(jnp.where(p < key, pairs, 0.0), axis=0, keepdims=True)
        slot = jnp.where(live > 0, 2.0 * base + rank, -1.0)
        slot_col = column(slot)
        first_hot = jnp.where(slot_col == 2.0 * lane, 1.0, 0.0)
        second_hot = jnp.where(slot_col == 2.0 * lane + 1.0, 1.0, 0.0)
        source_col = column(source)
        fresh_col = column(jnp.where(rank == 0.0, 1.0, 0.0))

        def pick(hot, v):
            return jnp.sum(hot * v, axis=0, keepdims=True)

        entry = sub[:, :1]
        a0 = pick(first_hot, entry - CAP) + CAP
        a1 = pick(second_hot, entry - CAP) + CAP
        before = jnp.sum(jnp.where(p < lane[:RB], pairs, 0.0), axis=0, keepdims=True)
        mine = jnp.sum(jnp.where(p == lane[:RB], pairs, 0.0), axis=0, keepdims=True)
        last = jnp.where(mine > 0, before + mine - 1.0, float(PAIRS))
        zero = jnp.zeros((1, CAP), F32)
        return [a0, a1, pick(first_hot, source_col), pick(second_hot, source_col), pick(first_hot, fresh_col), last, zero, zero]

    i = jnp.floor(cols * 0.25)
    x = jnp.floor(i * 0.25)
    yl = jnp.floor((i - 4.0 * x) * 0.5)
    c = i - 4.0 * x - 2.0 * yl
    col_place = (c * 8.0 + x * 2.0 + yl) * 4.0 + (cols - 4.0 * i)
    table = order(rows, col_place) + order(cols, rows)
    out_ref[...] = jnp.concatenate(table, axis=0).astype(jnp.int32)


def sort_lists(count, rows, cols):
    return pl.pallas_call(
        sort_kernel,
        out_shape=jax.ShapeDtypeStruct((16, CAP), jnp.int32),
        in_specs=[
            pl.BlockSpec(memory_space=pltpu.SMEM),
            pl.BlockSpec(memory_space=pltpu.VMEM),
            pl.BlockSpec(memory_space=pltpu.VMEM),
        ],
        out_specs=pl.BlockSpec(memory_space=pltpu.VMEM),
    )(count, rows, cols)


def gather_row_first(links, panel):
    yh, z, x, yl, c = place()
    xp, xm, xf, yo = rem(x + 1, 4), rem(x + 3, 4), rem(x + 2, 4), 1 - yl

    def at(at_x, at_y, first, n):
        return panel.at[pl.ds((c * 8 + at_x * 2 + at_y) * 4 + first, n)]

    over_y, sibling = device(yh, z, x, yo, c), device(yh, z, x, yl, 1 - c)
    around = [device(yh, z, xp, yl, c), device(yh, z, xm, yl, c), device(yh, z, xf, yl, c)]
    origin = (xm, xp, xf)

    def send(at_x, at_y, first, n, to):
        ref = at(at_x, at_y, first, n)
        return links.send(ref, ref, to)

    y_lo = send(x, yl, 0, 2, over_y)
    hi = [send(x, yl, 2, 2, to) for to in around]
    y_hi = send(x, yl, 2, 2, over_y)
    lo = [send(x, yl, 0, 2, to) for to in around]
    to_core = [send(x, yl, 0, 4, sibling)]
    yield
    y_lo.wait_recv()
    lo_other = [send(x, yo, 0, 2, to) for to in around]
    hi_other = []
    for n in range(3):
        hi[n].wait_recv()
        hi_other.append(send(origin[n], yl, 2, 2, over_y))
    yield
    y_hi.wait_recv()
    to_core.append(send(x, yo, 0, 4, sibling))
    for n in range(3):
        lo[n].wait_recv()
        to_core.append(send(origin[n], yl, 0, 4, sibling))
    yield
    for n in range(3):
        lo_other[n].wait_recv()
        hi_other[n].wait_recv()
        to_core.append(send(origin[n], yo, 0, 4, sibling))
    yield
    for copy in to_core:
        copy.wait_recv()


def gather_row(links, panel):
    yh, z, x, yl, c = place()
    xp, xm, yo, co = rem(x + 1, 4), rem(x + 3, 4), 1 - yl, 1 - c

    def one(at_x, at_y):
        return panel.at[pl.ds((c * 8 + at_x * 2 + at_y) * 4, 4)]

    def two(at_x):
        return panel.at[pl.ds((c * 8 + at_x * 2) * 4, 8)]

    right, left = device(yh, z, xp, yl, c), device(yh, z, xm, yl, c)
    over_y, sibling = device(yh, z, x, yo, c), device(yh, z, x, yl, co)
    mine, other = one(x, yl), one(x, yo)
    y_copy = links.send(mine, mine, over_y)
    r_mine = links.send(mine, mine, right)
    l_mine = links.send(mine, mine, left)
    to_core = [links.send(mine, mine, sibling)]
    yield
    y_copy.wait_recv()
    r_other = links.send(other, other, right)
    l_other = links.send(other, other, left)
    to_core.append(links.send(other, other, sibling))
    r_mine.wait_recv()
    r_far = links.send(one(xm, yl), one(xm, yl), right)
    yield
    l_other.wait_recv()
    l_far = links.send(one(xp, yo), one(xp, yo), left)
    r_other.wait_recv()
    to_core.append(links.send(two(xm), two(xm), sibling))
    l_mine.wait_recv()
    to_core.append(links.send(two(xp), two(xp), sibling))
    yield
    far = rem(x + 2, 4)
    r_far.wait_recv()
    to_core.append(links.send(one(far, yl), one(far, yl), sibling))
    l_far.wait_recv()
    to_core.append(links.send(one(far, yo), one(far, yo), sibling))
    yield
    for copy in to_core:
        copy.wait_recv()


def total(*terms):
    out = terms[0].astype(F32)
    for term in terms[1:]:
        out = out + term.astype(F32)
    return out


def own_rows(meta, sums, yh, z, o, block):
    p = (yh * 8 + rem(z + o, NZ)) * 4 + block
    return sums[meta[5, p]]


NEED = (4, 5, 3, 6, 2, 7, 1, 0)


def reduce_rep_a(links, meta, sums, ys, yr, ar, al, agg, h):
    yh, z, x, yl, c = place()
    up, down = device(yh, rem(z + 1, NZ), x, yl, c), device(yh, rem(z + NZ - 1, NZ), x, yl, c)
    over = device(1 - yh, z, x, yl, c)
    blocks = range(A_BLOCKS[h])
    y_copies = []
    for g in range(4):
        for n in (2 * g, 2 * g + 1):
            for k in blocks:
                ys[n, k] = own_rows(meta, sums, 1 - yh, z, NEED[n], k)
        part = pl.ds(2 * g, 2)
        y_copies.append(links.send(ys.at[part], yr.at[part], over))
    yield
    up_copy = down_copy = None
    for s in range(5):
        if s < 4:
            y_copies[s].wait_recv()
        if s > 0:
            up_copy.wait_recv()
        if s < 4:
            n = NEED.index(4 - s)
            for k in blocks:
                terms = [own_rows(meta, sums, yh, z, 4 - s, k), yr[n, k]]
                if s > 0:
                    terms.append(ar[s, k])
                ar[s, k] = total(*terms).astype(BF)
            up_copy = links.send(ar.at[s], ar.at[s + 1], up)
        if s > 0 and s < 4:
            down_copy.wait_recv()
        if s < 3:
            n = NEED.index(5 + s)
            for k in blocks:
                terms = [own_rows(meta, sums, yh, z, 5 + s, k), yr[n, k]]
                if s > 0:
                    terms.append(al[s, k])
                al[s, k] = total(*terms).astype(BF)
            down_copy = links.send(al.at[s], al.at[s + 1], down)
        yield
    n = NEED.index(0)
    for k in blocks:
        agg[pl.ds(k * B, B), pl.ds(h * B, B)] = total(
            own_rows(meta, sums, yh, z, 0, k), yr[n, k], ar[4, k], al[3, k]
        ).astype(BF)


def reduce_rep_b(links, meta, sums, br, bl, by, agg, h):
    yh, z, x, yl, c = place()
    up, down = device(yh, rem(z + 1, NZ), x, yl, c), device(yh, rem(z + NZ - 1, NZ), x, yl, c)
    over = device(1 - yh, z, x, yl, c)
    sides = (yh, 1 - yh)
    first = A_BLOCKS[h]
    blocks = range(4 - first)
    up_copy = down_copy = None
    for s in range(5):
        if s > 0:
            down_copy.wait_recv()
        if s < 4:
            for n in range(2):
                for k in blocks:
                    terms = [own_rows(meta, sums, sides[n], z, 4 + s, first + k)]
                    if s > 0:
                        terms.append(bl[s, n, k])
                    bl[s, n, k] = total(*terms).astype(BF)
            down_copy = links.send(bl.at[s], bl.at[s + 1], down)
        if s > 0 and s < 4:
            up_copy.wait_recv()
        if s < 3:
            for n in range(2):
                for k in blocks:
                    terms = [own_rows(meta, sums, sides[n], z, 3 - s, first + k)]
                    if s > 0:
                        terms.append(br[s, n, k])
                    br[s, n, k] = total(*terms).astype(BF)
            up_copy = links.send(br.at[s], br.at[s + 1], up)
        if s < 4:
            yield
    for k in blocks:
        by[0, k] = total(own_rows(meta, sums, 1 - yh, z, 0, first + k), bl[4, 1, k], br[3, 1, k]).astype(BF)
    y_copy = links.send(by.at[0], by.at[1], over)
    yield
    y_copy.wait_recv()
    for k in blocks:
        agg[pl.ds((first + k) * B, B), pl.ds(h * B, B)] = total(
            own_rows(meta, sums, yh, z, 0, first + k), bl[4, 0, k], br[3, 0, k], by[1, k]
        ).astype(BF)


def gather_rep_a(links, panel, h):
    yh, z, x, yl, c = place()
    up, down = device(yh, rem(z + 1, NZ), x, yl, c), device(yh, rem(z + NZ - 1, NZ), x, yl, c)
    over = device(1 - yh, z, x, yl, c)

    def at(o):
        return panel.at[pl.ds((yh * 8 + rem(z + NZ + o, NZ)) * 4, A_BLOCKS[h])]

    up_copy = links.send(at(0), at(0), up)
    down_copy = links.send(at(0), at(0), down)
    y_copies = [links.send(at(0), at(0), over)]
    yield
    for s in range(1, 5):
        up_copy.wait_recv()
        if s < 4:
            up_copy = links.send(at(-s), at(-s), up)
        y_copies.append(links.send(at(-s), at(-s), over))
        if s < 4:
            down_copy.wait_recv()
            if s < 3:
                down_copy = links.send(at(s), at(s), down)
            y_copies.append(links.send(at(s), at(s), over))
        yield
    for copy in y_copies:
        copy.wait_recv()


def gather_rep_b(links, panel, h):
    yh, z, x, yl, c = place()
    up, down = device(yh, rem(z + 1, NZ), x, yl, c), device(yh, rem(z + NZ - 1, NZ), x, yl, c)
    over = device(1 - yh, z, x, yl, c)
    first = A_BLOCKS[h]

    def at(side, o):
        return panel.at[pl.ds((side * 8 + rem(z + NZ + o, NZ)) * 4 + first, 4 - first)]

    y_copy = links.send(at(yh, 0), at(yh, 0), over)
    ups, downs = [None, None], [None, None]
    sides = (yh, 1 - yh)
    for s in range(0, 5):
        for n in range(2):
            if s == 0 and n == 1:
                yield
                y_copy.wait_recv()
            if s > 0:
                downs[n].wait_recv()
            if s < 4:
                downs[n] = links.send(at(sides[n], s), at(sides[n], s), down)
            if s > 0 and s < 4:
                ups[n].wait_recv()
            if s < 3:
                ups[n] = links.send(at(sides[n], -s), at(sides[n], -s), up)
        if s < 4:
            yield


ORDER = ((2, 1), (2, 0), (1, 1), (3, 1), (1, 0), (3, 0), (0, 1), (0, 0))


def reduce_row(links, meta, sums, cs, cr, stage, got, result, h):
    yh, z, x, yl, c = place()
    right, left = device(yh, z, rem(x + 1, 4), yl, c), device(yh, z, rem(x + 3, 4), yl, c)
    over_y, sibling = device(yh, z, x, 1 - yl, c), device(yh, z, x, yl, 1 - c)

    def own(core, dx, other, k):
        side = 1 - yl if other else yl
        q = (rem(x + dx, 4) * 4 + side * 2 + core) * 4 + k
        return sums[meta[13, q]]

    core_copies = []
    for g in range(4):
        for n in (2 * g, 2 * g + 1):
            for k in range(4):
                cs[n, k] = own(1 - c, *ORDER[n], k)
        part = pl.ds(2 * g, 2)
        core_copies.append(links.send(cs.at[part], cr.at[part], sibling))

    def both(dx, other, k):
        return (own(c, dx, other, k), cr[ORDER.index((dx, other)), k])

    slots = []

    def push(to, dx, other, blocks, *more):
        n = len(slots)
        slots.append(None)
        for at, k in enumerate(blocks):
            extra = [f(k) for f in more]
            stage[n, at] = total(*both(dx, other, k), *[e for e in extra if e is not None]).astype(BF)
        part = pl.ds(0, len(blocks))
        slots[n] = links.send(stage.at[n, part], got.at[n, part], to)
        return n

    def arrived(n, blocks):
        return lambda k: got[n, blocks.index(k)] if k in blocks else None

    lower, upper = (0, 1), (2, 3)
    yield
    core_copies[0].wait_recv()
    p_y2 = push(over_y, 2, 1, lower)
    q_r1 = push(right, 2, 0, upper)
    q_l1 = push(left, 2, 1, upper)
    core_copies[1].wait_recv()
    p_y1 = push(over_y, 1, 1, lower)
    p_y3 = push(over_y, 3, 1, lower)
    q_rp = push(right, 1, 1, upper)
    core_copies[2].wait_recv()
    q_lo = push(left, 3, 0, upper)
    core_copies[3].wait_recv()
    p_y0 = push(over_y, 0, 1, lower)
    yield
    slots[p_y2].wait_recv()
    p_r1 = push(right, 2, 0, (0,), arrived(p_y2, lower))
    p_l1 = push(left, 2, 0, (1,), arrived(p_y2, lower))
    slots[q_r1].wait_recv()
    q_r2 = push(right, 1, 0, upper, arrived(q_r1, upper))
    slots[q_l1].wait_recv()
    q_l2 = push(left, 3, 1, upper, arrived(q_l1, upper))
    yield
    slots[p_y1].wait_recv()
    slots[p_y3].wait_recv()
    slots[p_r1].wait_recv()
    p_r2 = push(right, 1, 0, lower, arrived(p_y1, lower), arrived(p_r1, (0,)))
    slots[p_l1].wait_recv()
    p_l2 = push(left, 3, 0, lower, arrived(p_y3, lower), arrived(p_l1, (1,)))
    slots[q_rp].wait_recv()
    slots[q_l2].wait_recv()
    q_y = push(over_y, 0, 1, upper, arrived(q_rp, upper), arrived(q_l2, upper))
    yield
    for n in (p_y0, p_r2, p_l2):
        slots[n].wait_recv()

    def finish(k, *terms):
        result[pl.ds(k * B, B), pl.ds(h * B, B)] = total(*both(0, 0, k), *terms).T.astype(BF)

    for k in lower:
        finish(k, got[p_y0, k], got[p_r2, k], got[p_l2, k])
    for n in (q_lo, q_r2, q_y):
        slots[n].wait_recv()
    for k in upper:
        finish(k, got[q_lo, k - 2], got[q_r2, k - 2], got[q_y, k - 2])


def reduce_weight(links, pieces, core_in, x_in, y_in, z_in, s1, s2, out):
    yh, z, x, yl, c = place()
    y = yh * 2 + yl
    sibling = device(yh, z, x, yl, 1 - c)
    up, down = device(yh, rem(z + 1, NZ), x, yl, c), device(yh, rem(z + NZ - 1, NZ), x, yl, c)
    other_x = [rem(x + d, 4) for d in range(1, 4)]
    other_y = [(yh, 1 - yl), (1 - yh, yl), (1 - yh, 1 - yl)]

    copy = links.send(pieces.at[pl.ds((1 - c) * 16, 16)], core_in, sibling)
    yield
    copy.wait_recv()
    s1[...] = pieces[pl.ds(c * 16, 16)] + core_in[...]
    copies = [links.send(s1.at[pl.ds(to * 4, 4)], x_in.at[n], device(yh, z, to, yl, c)) for n, to in enumerate(other_x)]
    yield
    for copy in copies:
        copy.wait_recv()
    s2[...] = s1[pl.ds(x * 4, 4)] + x_in[0] + x_in[1] + x_in[2]
    copies = [links.send(s2.at[a * 2 + b], y_in.at[n], device(a, z, x, b, c)) for n, (a, b) in enumerate(other_y)]
    yield
    for copy in copies:
        copy.wait_recv()
    z_in[z] = s2[y] + y_in[0] + y_in[1] + y_in[2]
    up_copy = links.send(z_in.at[z], z_in.at[z], up)
    down_copy = links.send(z_in.at[z], z_in.at[z], down)
    for s in range(1, 5):
        yield
        up_copy.wait_recv()
        if s < 4:
            spot = rem(z + NZ - s, NZ)
            up_copy = links.send(z_in.at[spot], z_in.at[spot], up)
            down_copy.wait_recv()
        if s < 3:
            spot = rem(z + s, NZ)
            down_copy = links.send(z_in.at[spot], z_in.at[spot], down)
    summed = z_in[0]
    for n in range(1, NZ):
        summed = summed + z_in[n]
    spot = c * 16 + x * 4 + y
    out[spot] = summed
    copies = [links.send(out.at[spot], out.at[spot], device(a, z, x, b, c)) for a, b in other_y]
    yield
    for copy in copies:
        copy.wait_recv()
    part = out.at[pl.ds(c * 16 + x * 4, 4)]
    copies = [links.send(part, part, device(yh, z, to, yl, c)) for to in other_x]
    yield
    for copy in copies:
        copy.wait_recv()
    part = out.at[pl.ds(c * 16, 16)]
    copy = links.send(part, part, sibling)
    yield
    copy.wait_recv()


A_BLOCKS = (3, 2)
COPIES = 256


def half_scratch(a):
    b = 4 - a
    forward = [
        (RB, B, B), (PAIRS + 1, B, B), (8, a, B, B), (8, a, B, B), (5, a, B, B), (4, a, B, B),
        (4, 2, b, B, B), (5, 2, b, B, B), (2, b, B, B),
    ]
    backward = [(RB, B, B), (8, 4, B, B), (8, 4, B, B), (15, 2, B, B), (15, 2, B, B)]
    return forward + backward


PIECES = [
    (32, 8, 384), (16, 8, 384), (3, 4, 8, 384), (3, 8, 384), (8, 8, 384), (16, 8, 384), (4, 8, 384), (32, 8, 384),
]


def layer_kernel(meta, feat_hbm, cot_hbm, weight, bias, adj_hbm, act, result, gw, gb, adj, *rest):
    halves = [rest[:14], rest[14:28]]
    piece_refs, (agg, grad, feat, cot, send_sem, recv_sem, local_sem) = rest[28:36], rest[36:]
    yh, z, x, yl, c = place()
    barrier = pltpu.get_barrier_semaphore()
    partners = [
        device(yh, rem(z + 1, NZ), x, yl, c), device(yh, rem(z + NZ - 1, NZ), x, yl, c),
        device(1 - yh, z, x, yl, c), device(yh, z, rem(x + 1, 4), yl, c), device(yh, z, rem(x + 3, 4), yl, c),
        device(yh, z, rem(x + 2, 4), yl, c), device(yh, z, x, 1 - yl, c), device(yh, z, x, yl, 1 - c),
        device(1 - yh, z, x, 1 - yl, c),
    ]
    for to in partners:
        pl.semaphore_signal(barrier, inc=1, device_id=to, device_id_type=MESH)
    links = Links(send_sem, recv_sem)
    feat_copy = pltpu.make_async_copy(feat_hbm, feat, local_sem.at[0])
    feat_copy.start()
    adj_copy = pltpu.make_async_copy(adj_hbm, adj.at[pl.ds(0, CAP)], local_sem.at[1])
    adj_copy.start()
    cot_copy = pltpu.make_async_copy(cot_hbm, cot, local_sem.at[2])
    cot_copy.start()
    adj[CAP] = jnp.zeros((B, B), BF)
    slot = (c * 8 + x * 2 + yl) * 4
    feat_copy.wait()
    for h in range(2):
        for k in range(4):
            halves[h][0][slot + k] = feat[pl.ds(k * B, B), pl.ds(h * B, B)]
    pl.semaphore_wait(barrier, len(partners))

    def reduces(h):
        panel, sums, ys, yr, ar, al, br, bl, by = halves[h][:9]
        return (
            reduce_rep_b(links, meta, sums, br, bl, by, agg, h),
            reduce_rep_a(links, meta, sums, ys, yr, ar, al, agg, h),
        )

    first, second = gather_row_first(links, halves[0][0]), gather_row(links, halves[1][0])
    advance(first, 3)
    next(second)
    run(first)
    adj_copy.wait()
    cot_copy.wait()
    work = products(meta, 0, adj, halves[0][0], halves[0][1], True)
    for n in range(8):
        next(work)
        if n == 1:
            next(second)
    b0, a0 = reduces(0)
    next(a0)
    next(b0)
    run(second)
    work = products(meta, 0, adj, halves[1][0], halves[1][1], True)
    for n in range(8):
        next(work)
        if n in (2, 6):
            next(b0)
        if n == 4:
            next(a0)
    b1, a1 = reduces(1)
    next(a1)
    next(b1)
    run(a0, b0, b1, a1)

    spot = (yh * 8 + z) * 4
    for k in range(4):
        rows = pl.ds(k * B, B)
        pre = jnp.dot(agg[rows, :], weight[...], preferred_element_type=F32) + bias[...]
        s = jax.nn.sigmoid(pre)
        act[rows, :] = (pre * s).astype(BF)
        grad_pre = (cot[rows, :].astype(F32) * (s * (1.0 + pre * (1.0 - s)))).astype(BF)
        grad[rows, :] = grad_pre
        back = lax.dot_general(weight[...], grad_pre, (((1,), (1,)), ((), ())), preferred_element_type=F32).astype(BF)
        for h in range(2):
            halves[h][9][spot + k] = back[h * B : (h + 1) * B]
    first, second = [
        together(gather_rep_b(links, halves[h][9], h), gather_rep_a(links, halves[h][9], h)) for h in range(2)
    ]
    advance(first, 2)
    gw_local = lax.dot_general(agg[...], grad[...], (((0,), (0,)), ((), ())), preferred_element_type=F32)
    gb_local = jnp.sum(grad[...].astype(F32), axis=0, keepdims=True)
    row = lax.broadcasted_iota(jnp.int32, (8, B), 0)
    bias_tile = jnp.where(row == 0, gb_local[:, :B], jnp.where(row == 1, gb_local[:, B:], 0.0))
    pieces, out = piece_refs[0], piece_refs[7]
    for n in range(32):
        pieces[n, :, 0:256] = gw_local[n * 8 : n * 8 + 8]
        pieces[n, :, 256:384] = bias_tile
    weights = reduce_weight(links, *piece_refs)
    next(weights)
    advance(first, 2)
    advance(second, 2)
    for n in range(7):
        next(first, None)
        if n in (1, 4):
            next(weights)
        if n in (3, 5):
            next(second)
    run(first)
    work = products(meta, 8, adj, halves[0][9], halves[0][1], False)
    for n in range(8):
        next(work)
        if n % 2 == 1:
            next(second)
        if n == 3:
            next(weights)

    def row_sums(h):
        return reduce_row(links, meta, halves[h][1], *halves[h][10:14], result, h)

    first = row_sums(0)
    next(first)
    next(second, None)
    next(first)
    next(weights)
    next(second, None)
    next(weights)
    next(second, None)
    next(first)
    run(second)
    next(weights)
    work = products(meta, 8, adj, halves[1][9], halves[1][1], False)
    for n in range(8):
        next(work)
        if n == 1:
            next(first, None)
        if n in (3, 6):
            next(weights)
    second = row_sums(1)
    run(second, weights, first)
    for n in range(32):
        gw[n * 8 : n * 8 + 8, :] = out[n, :, 0:256]
    gb[:, 0:B] = out[0, 0:1, 256:384]
    gb[:, B:256] = out[0, 1:2, 256:384]
    links.finish()


def layer(meta, feat, cot, weight, bias, adj):
    vmem = pl.BlockSpec(memory_space=pltpu.VMEM)
    anywhere = pl.BlockSpec(memory_space=pl.ANY)
    return pl.pallas_call(
        layer_kernel,
        out_shape=OUTS,
        in_specs=[pl.BlockSpec(memory_space=pltpu.SMEM), anywhere, anywhere, vmem, vmem, anywhere],
        out_specs=(vmem, vmem, vmem, vmem),
        scratch_shapes=[pltpu.VMEM((CAP + 1, B, B), BF)]
        + [pltpu.VMEM(shape, BF) for a in A_BLOCKS for shape in half_scratch(a)]
        + [pltpu.VMEM(shape, F32) for shape in PIECES]
        + [
            pltpu.VMEM((512, 256), BF),
            pltpu.VMEM((512, 256), BF),
            pltpu.VMEM((512, 256), BF),
            pltpu.VMEM((512, 256), BF),
            pltpu.SemaphoreType.DMA((COPIES,)),
            pltpu.SemaphoreType.DMA((COPIES,)),
            pltpu.SemaphoreType.DMA((3,)),
        ],
        compiler_params=pltpu.CompilerParams(collective_id=1, has_side_effects=True, vmem_limit_bytes=VMEM_LIMIT),
    )(meta, feat, cot, weight, bias, adj)


OUTS = (
    jax.ShapeDtypeStruct((512, 256), BF),
    jax.ShapeDtypeStruct((512, 256), BF),
    jax.ShapeDtypeStruct((256, 256), F32),
    jax.ShapeDtypeStruct((1, 256), F32),
)


def hand_over_kernel(*refs):
    given, results, held, sem = refs[:4], refs[4:8], refs[8:12], refs[12]
    arrive = [pltpu.make_async_copy(given[n], held[n], sem.at[n]) for n in range(4)]
    leave = [pltpu.make_async_copy(held[n], results[n], sem.at[4 + n]) for n in range(4)]
    for copy in arrive:
        copy.start()
    for n in range(4):
        arrive[n].wait()
        leave[n].start()
    for copy in leave:
        copy.wait()


def hand_over(*arrays):
    outside = pl.BlockSpec(memory_space=pltpu.HBM)
    return pl.pallas_call(
        hand_over_kernel,
        out_shape=OUTS,
        in_specs=[outside] * 4,
        out_specs=(outside,) * 4,
        scratch_shapes=[pltpu.VMEM(out.shape, out.dtype) for out in OUTS] + [pltpu.SemaphoreType.DMA((8,))],
    )(*arrays)


def per_device(features, adj_values, block_rows, block_cols, counts, weight, bias, cotangent):
    adj = adj_values.reshape(CAP, B, B)
    meta = sort_lists(counts, block_rows.reshape(1, CAP), block_cols.reshape(1, CAP))
    act, result, gw, gb = hand_over(*layer(meta, features, cotangent, weight, bias.reshape(1, 256), adj))
    return act, result, gw, gb.reshape(256)


def solution(mesh):
    return jax.shard_map(
        per_device,
        mesh=mesh,
        in_specs=(
            P(("rep", "row"), None),
            P("rep", "row", None, None, None),
            P("rep", "row", None),
            P("rep", "row", None),
            P("rep", "row"),
            P(),
            P(),
            P(("rep", "row"), None),
        ),
        out_specs=(P(("rep", "row"), None), P(("rep", "row"), None), P(), P()),
        check_vma=False,
    )
```

profile of v0, /device:TPU:6, one launch (start us, length us, event | category | flops | bytes accessed | tf_op | source)
XLA Modules:
  0.0 146.2 jit_solution(2085372422661524336)
XLA Ops:
  1.3 2.0 %shard_map.111.meta = s32[16,256]{1,0:T(8,128)} custom-call(s32[1,1]{1,0:T(1,128)S(6)} %copy.12.count_ref, s32[1,256]{1,0:T(1,128)} %bitcast.7, s32[1,256]{1,0:T(1,128)} %bitcast.8), custom_call_target="tpu_custom_call" | custom-call | tf_op jit(solution)/shard_map/pallas_call | solution.py:152
  3.2 140.9 %shard_map.112 = (bf16[512,256]{1,0:T(8,128)(2,1)}, bf16[512,256]{1,0:T(8,128)(2,1)}, f32[256,256]{1,0:T(8,128)}, f32[1,256]{1,0:T(1,128)}) custom-call(s32[16,256]{1,0:T(8,128)} %shard_map.111.meta, bf16[512,256]{1,0:T(8,128)(2,1)} %feat_hbm.1, bf16[512,256]{1,0:T(8,128)(2,1)} %cot_hbm.1, bf16[256,256]{1,0:T(8,128)(2,1)} %weight.1, f32[1,256]{1,0:T(1,128)} %bitcast.6, ...), custom_call_target="tpu_custom_call" | custom-call | tf_op jit(solution)/shard_map/pallas_call | solution.py:703
  144.2 1.9 %shard_map.113 = (bf16[512,256]{1,0:T(8,128)(2,1)}, bf16[512,256]{1,0:T(8,128)(2,1)}, f32[256,256]{1,0:T(8,128)}, f32[1,256]{1,0:T(1,128)}) custom-call(bf16[512,256]{1,0:T(8,128)(2,1)} %get-tuple-element.12.refs_0_, bf16[512,256]{1,0:T(8,128)(2,1)} %get-tuple-element.13.refs_1_, f32[256,256]{1,0:T(8,128)} %get-tuple-element.14.refs_2_, ...), custom_call_target="tpu_custom_call" | custom-call | tf_op jit(solution)/shard_map/pallas_call | solution.py:747
where the time goes:
time: 146 us
  Pallas kernels  145 us (99%)
    pallas_call x1, Pallas kernels, layer(): pl.pallas_call(layer_kernel, out_shape=OUTS, in_specs=[pl.BlockSpec(memor...  141 us

commit v1 on v0

--- a/solution.py
+++ b/solution.py
@@ -75,10 +75,14 @@
         next(task, None)
 
 
+def entry(meta, row, n, top):
+    return jnp.minimum(jnp.maximum(meta[row, n], 0), top)
+
+
 def products(meta, base, adj, source, sums, adj_first):
     def step(t, acc):
-        a0, a1 = adj[meta[base, t]], adj[meta[base + 1, t]]
-        x0, x1 = source[meta[base + 2, t]], source[meta[base + 3, t]]
+        a0, a1 = adj[entry(meta, base, t, CAP)], adj[entry(meta, base + 1, t, CAP)]
+        x0, x1 = source[entry(meta, base + 2, t, RB - 1)], source[entry(meta, base + 3, t, RB - 1)]
         if adj_first:
             left, right = jnp.concatenate([a0, a1], 1), jnp.concatenate([x0, x1], 0)
         else:
@@ -100,7 +104,7 @@
         yield
 
 
-def sort_kernel(count_ref, rows_ref, cols_ref, out_ref):
+def sort_lists(count_ref, rows_ref, cols_ref, out_ref):
     live = (lax.broadcasted_iota(jnp.int32, (1, CAP), 1) < count_ref[0, 0]).astype(F32)
     sub = lax.broadcasted_iota(jnp.int32, (CAP, CAP), 0).astype(F32)
     lane = lax.broadcasted_iota(jnp.int32, (CAP, CAP), 1).astype(F32)
@@ -148,19 +152,6 @@
     out_ref[...] = jnp.concatenate(table, axis=0).astype(jnp.int32)
 
 
-def sort_lists(count, rows, cols):
-    return pl.pallas_call(
-        sort_kernel,
-        out_shape=jax.ShapeDtypeStruct((16, CAP), jnp.int32),
-        in_specs=[
-            pl.BlockSpec(memory_space=pltpu.SMEM),
-            pl.BlockSpec(memory_space=pltpu.VMEM),
-            pl.BlockSpec(memory_space=pltpu.VMEM),
-        ],
-        out_specs=pl.BlockSpec(memory_space=pltpu.VMEM),
-    )(count, rows, cols)
-
-
 def gather_row_first(links, panel):
     yh, z, x, yl, c = place()
     xp, xm, xf, yo = rem(x + 1, 4), rem(x + 3, 4), rem(x + 2, 4), 1 - yl
@@ -255,7 +246,7 @@
 
 def own_rows(meta, sums, yh, z, o, block):
     p = (yh * 8 + rem(z + o, NZ)) * 4 + block
-    return sums[meta[5, p]]
+    return sums[entry(meta, 5, p, PAIRS)]
 
 
 NEED = (4, 5, 3, 6, 2, 7, 1, 0)
@@ -415,7 +406,7 @@
     def own(core, dx, other, k):
         side = 1 - yl if other else yl
         q = (rem(x + dx, 4) * 4 + side * 2 + core) * 4 + k
-        return sums[meta[13, q]]
+        return sums[entry(meta, 13, q, PAIRS)]
 
     core_copies = []
     for g in range(4):
@@ -563,9 +554,9 @@
 ]
 
 
-def layer_kernel(meta, feat_hbm, cot_hbm, weight, bias, adj_hbm, act, result, gw, gb, adj, *rest):
+def layer_kernel(count, list_rows, list_cols, feat_hbm, cot_hbm, weight, bias, adj_hbm, act, result, gw, gb, adj, *rest):
     halves = [rest[:14], rest[14:28]]
-    piece_refs, (agg, grad, feat, cot, send_sem, recv_sem, local_sem) = rest[28:36], rest[36:]
+    piece_refs, (agg, grad, feat, cot, table, meta, send_sem, recv_sem, local_sem) = rest[28:36], rest[36:]
     yh, z, x, yl, c = place()
     barrier = pltpu.get_barrier_semaphore()
     partners = [
@@ -589,6 +580,9 @@
     for h in range(2):
         for k in range(4):
             halves[h][0][slot + k] = feat[pl.ds(k * B, B), pl.ds(h * B, B)]
+    sort_lists(count, list_rows, list_cols, table)
+    meta_copy = pltpu.make_async_copy(table, meta, local_sem.at[3])
+    meta_copy.start()
     pl.semaphore_wait(barrier, len(partners))
 
     def reduces(h):
@@ -602,6 +596,7 @@
     advance(first, 3)
     next(second)
     run(first)
+    meta_copy.wait()
     adj_copy.wait()
     cot_copy.wait()
     work = products(meta, 0, adj, halves[0][0], halves[0][1], True)
@@ -639,7 +634,13 @@
     first, second = [
         together(gather_rep_b(links, halves[h][9], h), gather_rep_a(links, halves[h][9], h)) for h in range(2)
     ]
-    advance(first, 2)
+    tasks = dict(F=first, S=second)
+
+    def follow(order):
+        for name in order:
+            next(tasks[name], None)
+
+    follow("FFSS")
     gw_local = lax.dot_general(agg[...], grad[...], (((0,), (0,)), ((), ())), preferred_element_type=F32)
     gb_local = jnp.sum(grad[...].astype(F32), axis=0, keepdims=True)
     row = lax.broadcasted_iota(jnp.int32, (8, B), 0)
@@ -648,48 +649,21 @@
     for n in range(32):
         pieces[n, :, 0:256] = gw_local[n * 8 : n * 8 + 8]
         pieces[n, :, 256:384] = bias_tile
-    weights = reduce_weight(links, *piece_refs)
-    next(weights)
-    advance(first, 2)
-    advance(second, 2)
-    for n in range(7):
-        next(first, None)
-        if n in (1, 4):
-            next(weights)
-        if n in (3, 5):
-            next(second)
-    run(first)
-    work = products(meta, 8, adj, halves[0][9], halves[0][1], False)
-    for n in range(8):
-        next(work)
-        if n % 2 == 1:
-            next(second)
-        if n == 3:
-            next(weights)
 
     def row_sums(h):
         return reduce_row(links, meta, halves[h][1], *halves[h][10:14], result, h)
 
-    first = row_sums(0)
-    next(first)
-    next(second, None)
-    next(first)
-    next(weights)
-    next(second, None)
-    next(weights)
-    next(second, None)
-    next(first)
-    run(second)
-    next(weights)
-    work = products(meta, 8, adj, halves[1][9], halves[1][1], False)
-    for n in range(8):
-        next(work)
-        if n == 1:
-            next(first, None)
-        if n in (3, 6):
-            next(weights)
-    second = row_sums(1)
-    run(second, weights, first)
+    tasks["W"] = reduce_weight(links, *piece_refs)
+    tasks["P"] = products(meta, 8, adj, halves[0][9], halves[0][1], False)
+    tasks["R"] = row_sums(0)
+    follow("WFFSWFFSSWFSFSWFSF")
+    run(first)
+    follow("PSPSWPSPSPPWPPRR")
+    run(tasks["P"], second)
+    tasks["P"] = products(meta, 8, adj, halves[1][9], halves[1][1], False)
+    follow("WPPRPWPPRWPPRWP")
+    run(tasks["P"])
+    run(row_sums(1), tasks["W"], tasks["R"])
     for n in range(32):
         gw[n * 8 : n * 8 + 8, :] = out[n, :, 0:256]
     gb[:, 0:B] = out[0, 0:1, 256:384]
@@ -697,13 +671,13 @@
     links.finish()
 
 
-def layer(meta, feat, cot, weight, bias, adj):
+def layer(count, rows, cols, feat, cot, weight, bias, adj):
     vmem = pl.BlockSpec(memory_space=pltpu.VMEM)
     anywhere = pl.BlockSpec(memory_space=pl.ANY)
     return pl.pallas_call(
         layer_kernel,
         out_shape=OUTS,
-        in_specs=[pl.BlockSpec(memory_space=pltpu.SMEM), anywhere, anywhere, vmem, vmem, anywhere],
+        in_specs=[pl.BlockSpec(memory_space=pltpu.SMEM), vmem, vmem, anywhere, anywhere, vmem, vmem, anywhere],
         out_specs=(vmem, vmem, vmem, vmem),
         scratch_shapes=[pltpu.VMEM((CAP + 1, B, B), BF)]
         + [pltpu.VMEM(shape, BF) for a in A_BLOCKS for shape in half_scratch(a)]
@@ -713,12 +687,14 @@
             pltpu.VMEM((512, 256), BF),
             pltpu.VMEM((512, 256), BF),
             pltpu.VMEM((512, 256), BF),
+            pltpu.VMEM((16, CAP), jnp.int32),
+            pltpu.SMEM((16, CAP), jnp.int32),
             pltpu.SemaphoreType.DMA((COPIES,)),
             pltpu.SemaphoreType.DMA((COPIES,)),
-            pltpu.SemaphoreType.DMA((3,)),
+            pltpu.SemaphoreType.DMA((4,)),
         ],
         compiler_params=pltpu.CompilerParams(collective_id=1, has_side_effects=True, vmem_limit_bytes=VMEM_LIMIT),
-    )(meta, feat, cot, weight, bias, adj)
+    )(count, rows, cols, feat, cot, weight, bias, adj)
 
 
 OUTS = (
@@ -755,8 +731,10 @@
 
 def per_device(features, adj_values, block_rows, block_cols, counts, weight, bias, cotangent):
     adj = adj_values.reshape(CAP, B, B)
-    meta = sort_lists(counts, block_rows.reshape(1, CAP), block_cols.reshape(1, CAP))
-    act, result, gw, gb = hand_over(*layer(meta, features, cotangent, weight, bias.reshape(1, 256), adj))
+    rows, cols = block_rows.reshape(1, CAP), block_cols.reshape(1, CAP)
+    act, result, gw, gb = hand_over(
+        *layer(counts, rows, cols, features, cotangent, weight, bias.reshape(1, 256), adj)
+    )
     return act, result, gw, gb.reshape(256)
 
 

time: 146 us -> 143 us (0.979)
  Pallas kernels: 145 us -> 142 us
    pallas_call x1 -> x0, Pallas kernels: 1.95 us -> none  [sort_lists(): pl.pallas_call(sort_kernel, out_shape=jax.ShapeDtypeStruct((16, CAP), jnp...]
where the time goes in v1:
time: 143 us
  Pallas kernels  142 us (99%)
  between operations  1.45 us (1%)
    pallas_call x1, Pallas kernels, layer(): pl.pallas_call(layer_kernel, out_shape=OUTS, in_specs=[pl.BlockSpec(memor...  140 us

profile of v1, /device:TPU:6, one launch (start us, length us, event | category | flops | bytes accessed | tf_op | source)
XLA Modules:
  0.0 143.1 jit_solution(22798587400236444)
XLA Ops:
  1.3 139.8 %shard_map.111 = (bf16[512,256]{1,0:T(8,128)(2,1)}, bf16[512,256]{1,0:T(8,128)(2,1)}, f32[256,256]{1,0:T(8,128)}, f32[1,256]{1,0:T(1,128)}) custom-call(s32[1,1]{1,0:T(1,128)S(6)} %copy.12.count, s32[1,256]{1,0:T(1,128)} %bitcast.6, s32[1,256]{1,0:T(1,128)} %bitcast.7, bf16[512,256]{1,0:T(8,128)(2,1)} %feat_hbm.1, bf16[512,256]{1,0:T(8,128)(2,1)} %cot_hbm.1, ...), custom_call_target="tpu_custom_call" | custom-call | tf_op jit(solution)/shard_map/pallas_call | solution.py:677
  141.0 1.9 %shard_map.112 = (bf16[512,256]{1,0:T(8,128)(2,1)}, bf16[512,256]{1,0:T(8,128)(2,1)}, f32[256,256]{1,0:T(8,128)}, f32[1,256]{1,0:T(1,128)}) custom-call(bf16[512,256]{1,0:T(8,128)(2,1)} %get-tuple-element.12.refs_0_, bf16[512,256]{1,0:T(8,128)(2,1)} %get-tuple-element.13.refs_1_, f32[256,256]{1,0:T(8,128)} %get-tuple-element.14.refs_2_, ...), custom_call_target="tpu_custom_call" | custom-call | tf_op jit(solution)/shard_map/pallas_call | solution.py:723
